TPU v7x, 32 devices: a whole 2x2x4 slice. The times are simulated.
32 devices in a mesh: group: 4 (over z), member: 8 (over y, x, core).
Axes of the slice: x: 2, y: 2, z: 4, core: 2. Of those that a mesh axis runs over, the one named last changes fastest.
Arguments:
- tokens: bfloat16 [32, 3584], P(('group', 'member')), may hold values from -6 to 6
- grad_out: bfloat16 [32, 3584], P(('group', 'member')), may hold values from -6 to 6
- route_token: int32 [4, 4, 1, 8], P('group'), may hold values from 0 to 7, as said below
- route_count: int32 [4, 4, 1], P('group'), may hold values from 0 to 8, as said below
- route_prob: float32 [4, 4, 1, 8], P('group'), may hold values from 0.05 to 0.6
- w_gate: bfloat16 [32, 128, 3584], P(('group', 'member')), may hold values from -0.09375 to 0.09375
- w_up: bfloat16 [32, 128, 3584], P(('group', 'member')), may hold values from -0.09375 to 0.09375
- w_down: bfloat16 [32, 128, 3584], P(('group', 'member')), may hold values from -0.1875 to 0.1875
Outputs:
- grad_tokens: bfloat16 [32, 3584], P(('group', 'member'))
- grad_gate: bfloat16 [32, 128, 3584], P(('group', 'member'))
- grad_up: bfloat16 [32, 128, 3584], P(('group', 'member'))
- grad_down: bfloat16 [32, 128, 3584], P(('group', 'member'))
Inputs may be any that keep to these rules, and one draw needn't show every extreme that they name: Each token of a source group is routed to 1 different experts in each of 2 different groups. An expert keeps, for each source group, the first 8 of the tokens routed to it in token order and drops the rest; route_token lists the kept tokens in that order, all different, and slots at or past route_count hold 0. In every draw one expert keeps 8 tokens from every source group. `route_count`: the number of kept tokens of each source group for each expert; 8 is reached in every draw.
All inputs are finite; a program needn't handle non-finite values.
Results may differ from a plain program's by a relative error of at most 0.0058.
Values may be sent and summed in bfloat16 or wider, within the bound.
No kernel may reach another device: no remote copies, remote signals or barrier semaphores. Data moves between devices by JAX's collectives and lax.ppermute only.
A program may use at most 64 MiB of HBM per device.

v0:
```python
import functools

import jax
import jax.numpy as jnp
from jax import lax
from jax.experimental import pallas as pl
from jax.experimental.pallas import tpu as pltpu
from jax.sharding import PartitionSpec as P

LANES = 128
PARTS = 4
AXES = ("group", "member")
VMEM = pl.BlockSpec(memory_space=pltpu.VMEM)
HBM = pl.BlockSpec(memory_space=pltpu.HBM)
SMEM = pl.BlockSpec(memory_space=pltpu.SMEM)
NT = (((1,), (1,)), ((), ()))
TN = (((0,), (0,)), ((), ()))


def pack_kernel(
    chunks,
    tokens_hbm,
    grad_hbm,
    token_hbm,
    count_hbm,
    prob_hbm,
    out_ref,
    rows_ref,
    tokens_ref,
    grad_ref,
    token_ref,
    count_ref,
    prob_ref,
    sems,
):
    pairs = (
        (token_hbm, token_ref),
        (count_hbm, count_ref),
        (prob_hbm, prob_ref),
        (tokens_hbm, tokens_ref),
        (grad_hbm, grad_ref),
    )
    copies = [pltpu.make_async_copy(*pair, sems.at[n]) for n, pair in enumerate(pairs)]
    for copy in copies:
        copy.start()
    for copy in copies:
        copy.wait()
    me = lax.axis_index("member")
    groups, _, capacity = token_ref.shape[1:]
    token_row = tokens_ref[...].astype(jnp.float32)
    grad_row = grad_ref[...].astype(jnp.float32)
    for k in range(chunks):
        part = slice(k * LANES, (k + 1) * LANES)
        rows_ref[k : k + 1, :] = token_row[:, part]
        rows_ref[chunks + k : chunks + k + 1, :] = grad_row[:, part]
    rows = rows_ref[...]
    is_token = lax.broadcasted_iota(jnp.int32, rows.shape, 0) < chunks
    places = out_ref.shape[0] // groups
    for g in range(groups):
        weight = jnp.float32(0)
        for p in range(capacity):
            live = (token_ref[0, g, 0, p] == me) & (p < count_ref[0, 0, g])
            weight = weight + jnp.where(live, prob_ref[0, g, 0, p], 0.0)
        packed = jnp.where(is_token, rows, rows * weight).astype(jnp.bfloat16)
        for n in range(places):
            out_ref[g * places + n] = packed


def unpack_rows(chunks, packed_ref, wide_ref, rows_ref):
    tokens, rows, _ = packed_ref.shape
    wide_ref[...] = packed_ref[...].astype(jnp.float32).reshape(tokens * rows, LANES)
    for k in range(rows):
        column = wide_ref[pl.ds(k, tokens, stride=rows), :]
        rows_ref[:, k * LANES : (k + 1) * LANES] = column.astype(jnp.bfloat16)


def unpack_kernel(chunks, mine_ref, rows_ref, wide_ref):
    unpack_rows(chunks, mine_ref, wide_ref, rows_ref)


def partial_kernel(
    chunks,
    mine_ref,
    other_ref,
    gate_ref,
    up_ref,
    down_ref,
    sent_ref,
    rows_ref,
    acts_ref,
    wide_ref,
    spread_ref,
):
    count = mine_ref.shape[0]
    tokens = 2 * count
    features = chunks * LANES
    units = gate_ref.shape[1]
    rows_ref[:count] = mine_ref[...]
    unpack_rows(chunks, other_ref, wide_ref, rows_ref.at[pl.ds(count, count)])
    x, scaled = rows_ref[:, :features], rows_ref[:, features:]
    both = jnp.concatenate([gate_ref[0], up_ref[0]], axis=0)
    values = lax.dot_general(both, x, NT, preferred_element_type=jnp.float32)
    gate_value, up_value = values[:units], values[units:]
    d_hidden = lax.dot_general(down_ref[0], scaled, NT, preferred_element_type=jnp.float32)
    sigma_gate = jax.nn.sigmoid(gate_value)
    active = gate_value * sigma_gate
    d_gate = d_hidden * up_value * sigma_gate * (1.0 + gate_value * (1.0 - sigma_gate))
    acts_ref[0:units] = d_gate.astype(jnp.bfloat16)
    acts_ref[units : 2 * units] = (d_hidden * active).astype(jnp.bfloat16)
    acts_ref[2 * units :] = (active * up_value).astype(jnp.bfloat16)
    partial = lax.dot_general(
        acts_ref[: 2 * units], both, TN, preferred_element_type=jnp.float32
    )
    blocks, height = sent_ref.shape[2:4]
    sent_rows = blocks * height
    for k in range(chunks):
        spread_ref[pl.ds(k, tokens, stride=sent_rows), :] = partial[:, k * LANES : (k + 1) * LANES]
    core = lax.rem(lax.axis_index("member"), 2)
    for n in range(2):
        for i in range(count):
            for k in range(blocks):
                first = (n * count + i) * sent_rows + k * height
                sent_ref[i, core ^ n, k] = spread_ref[first : first + height, :].astype(jnp.bfloat16)


def grads_kernel(
    features, rows_ref, acts_ref, gate_out, up_out, down_out, held_ref, sems
):
    units = held_ref.shape[1]
    height = units // PARTS
    copies = []
    for n, (out, first) in enumerate(((gate_out, 0), (up_out, 0), (down_out, features))):
        right = rows_ref[:, first : first + features]
        for k in range(PARTS):
            left = acts_ref[n * units + k * height : n * units + (k + 1) * height, :]
            held_ref[n, k * height : (k + 1) * height] = jnp.dot(
                left, right, preferred_element_type=jnp.float32
            ).astype(jnp.bfloat16)
            part = pl.ds(k * height, height)
            copies.append(
                pltpu.make_async_copy(held_ref.at[n, part], out.at[0, part], sems.at[PARTS * n + k])
            )
            copies[-1].start()
    for copy in copies:
        copy.wait()


def sum_kernel(back_ref, out_ref):
    count, blocks, height, _ = back_ref.shape
    for k in range(blocks):
        total = back_ref[0, k].astype(jnp.float32)
        for n in range(1, count):
            total = total + back_ref[n, k].astype(jnp.float32)
        for r in range(height):
            part = pl.ds((k * height + r) * LANES, LANES)
            out_ref[:, part] = total[r : r + 1, :].astype(jnp.bfloat16)


def exchange(value, distance):
    count = lax.axis_size("group") * lax.axis_size("member")
    return lax.ppermute(value, AXES, [(i, i ^ distance) for i in range(count)])


def in_hbm(value):
    return pltpu.with_memory_space_constraint(value, pltpu.HBM)


def dense_shards(tokens, grad_out, route_token, route_count, route_prob, w_gate, w_up, w_down):
    features = tokens.shape[1]
    units = w_gate.shape[1]
    chunks = features // LANES
    count = lax.axis_size("group") * lax.axis_size("member")
    half = count // 2
    rows = 2 * chunks
    arguments = (tokens, grad_out, route_token, jnp.swapaxes(route_count, 1, 2), route_prob)
    spaces = (pltpu.VMEM, pltpu.VMEM, pltpu.SMEM, pltpu.SMEM, pltpu.SMEM)
    copies = pl.pallas_call(
        functools.partial(pack_kernel, chunks),
        out_shape=pltpu.VMEM((half, rows, LANES), jnp.bfloat16),
        in_specs=[HBM] * 5,
        out_specs=VMEM,
        scratch_shapes=[pltpu.VMEM((rows, LANES), jnp.float32)]
        + [space(value.shape, value.dtype) for space, value in zip(spaces, arguments)]
        + [pltpu.SemaphoreType.DMA((5,))],
        compiler_params=pltpu.CompilerParams(vmem_limit_bytes=4 * 1024 * 1024),
        cost_estimate=pl.CostEstimate(
            flops=40000 * units * features,
            bytes_accessed=16 * units * features,
            transcendentals=0,
        ),
        name="pack_rows",
    )(*[in_hbm(value) for value in arguments])
    cores = [list(range(c, count, 2)) for c in range(2)]
    trade = functools.partial(
        lax.all_to_all,
        axis_name=AXES,
        split_axis=0,
        concat_axis=0,
        tiled=True,
        axis_index_groups=cores,
    )
    mine = trade(copies)
    other = exchange(mine, 1)
    wide = pltpu.VMEM((half * rows, LANES), jnp.float32)
    unpacked = pl.pallas_call(
        functools.partial(unpack_kernel, chunks),
        out_shape=pltpu.VMEM((half, 2 * features), jnp.bfloat16),
        in_specs=[VMEM],
        out_specs=VMEM,
        scratch_shapes=[wide],
        compiler_params=pltpu.CompilerParams(vmem_limit_bytes=2 * 1024 * 1024),
        name="unpack_rows",
    )(mine)
    sent, both, acts = pl.pallas_call(
        functools.partial(partial_kernel, chunks),
        out_shape=(
            jax.ShapeDtypeStruct((half, 2, chunks // 4, 4, LANES), jnp.bfloat16),
            pltpu.VMEM((count, 2 * features), jnp.bfloat16),
            pltpu.VMEM((3 * units, count), jnp.bfloat16),
        ),
        in_specs=[VMEM] * 5,
        out_specs=(VMEM,) * 3,
        scratch_shapes=[wide, pltpu.VMEM((count * chunks, LANES), jnp.float32)],
        compiler_params=pltpu.CompilerParams(vmem_limit_bytes=16 * 1024 * 1024),
        name="partial_rows",
    )(unpacked, other, w_gate, w_up, w_down)
    grad_shape = jax.ShapeDtypeStruct((1, units, features), jnp.bfloat16)
    grad_gate, grad_up, grad_down = pl.pallas_call(
        functools.partial(grads_kernel, features),
        out_shape=(grad_shape,) * 3,
        in_specs=[VMEM] * 2,
        out_specs=(HBM, HBM, HBM),
        scratch_shapes=[
            pltpu.VMEM((3, units, features), jnp.bfloat16),
            pltpu.SemaphoreType.DMA((3 * PARTS,)),
        ],
        compiler_params=pltpu.CompilerParams(vmem_limit_bytes=16 * 1024 * 1024),
        cost_estimate=pl.CostEstimate(
            flops=6 * count * units * features,
            bytes_accessed=6 * units * features,
            transcendentals=0,
        ),
        name="weight_grads",
    )(both, acts)
    back = lax.all_to_all(
        sent.reshape(count, chunks // 4, 4, LANES), AXES, 0, 0, tiled=True
    )
    grad_tokens = pl.pallas_call(
        sum_kernel,
        out_shape=jax.ShapeDtypeStruct((1, features), jnp.bfloat16),
        in_specs=[VMEM],
        out_specs=VMEM,
        compiler_params=pltpu.CompilerParams(vmem_limit_bytes=4 * 1024 * 1024),
        name="sum_rows",
    )(back)
    return grad_tokens, grad_gate, grad_up, grad_down


def slice_backward(rows_x, rows_scaled, gate_weight, up_weight, down_weight):
    gate_value = jnp.dot(rows_x, gate_weight.T, preferred_element_type=jnp.float32)
    up_value = jnp.dot(rows_x, up_weight.T, preferred_element_type=jnp.float32)
    sigma_gate = jax.nn.sigmoid(gate_value)
    active = gate_value * sigma_gate
    hidden = (active * up_value).astype(jnp.bfloat16)
    d_hidden = jnp.dot(rows_scaled, down_weight.T, preferred_element_type=jnp.float32)
    d_gate = (d_hidden * up_value * sigma_gate * (1.0 + gate_value * (1.0 - sigma_gate))).astype(
        jnp.bfloat16
    )
    d_up = (d_hidden * active).astype(jnp.bfloat16)
    grad_down = jnp.dot(hidden.T, rows_scaled, preferred_element_type=jnp.float32).astype(
        jnp.bfloat16
    )
    grad_gate = jnp.dot(d_gate.T, rows_x, preferred_element_type=jnp.float32).astype(jnp.bfloat16)
    grad_up = jnp.dot(d_up.T, rows_x, preferred_element_type=jnp.float32).astype(jnp.bfloat16)
    partial_rows = jnp.dot(d_gate, gate_weight, preferred_element_type=jnp.float32)
    partial_rows = partial_rows + jnp.dot(d_up, up_weight, preferred_element_type=jnp.float32)
    return (grad_gate, grad_up, grad_down, partial_rows)


def routed_shards(tokens, grad_out, route_token, route_count, route_prob, w_gate, w_up, w_down):
    groups = route_token.shape[1]
    capacity = route_token.shape[3]
    features = tokens.shape[1]
    block_rows = groups * capacity
    split_count = max(8, lax.axis_size("member") // 8)
    expert_local = lax.axis_index("member") // split_count
    slot_tokens = lax.dynamic_index_in_dim(route_token[0], expert_local, 1, keepdims=False)
    slot_counts = lax.dynamic_index_in_dim(route_count[0], expert_local, 1, keepdims=False)
    slot_probs = lax.dynamic_index_in_dim(route_prob[0], expert_local, 1, keepdims=False)
    slot_index = jnp.arange(capacity, dtype=jnp.int32)[None, :]
    live = (slot_index < slot_counts[:, None]).astype(jnp.float32)
    slot_weights = (slot_probs * live).reshape(-1)
    flat_slots = slot_tokens.reshape(-1)
    group_x, group_dy = (
        lax.all_gather(tokens, "member", axis=0, tiled=True),
        lax.all_gather(grad_out, "member", axis=0, tiled=True),
    )
    picked_x = jnp.take(group_x, flat_slots, axis=0)
    picked_dy = jnp.take(group_dy, flat_slots, axis=0)
    scaled = (slot_weights[:, None] * picked_dy.astype(jnp.float32)).astype(jnp.bfloat16)
    send_x = picked_x.reshape(groups, capacity, features)
    send_scaled = scaled.reshape(groups, capacity, features)
    rows_x, rows_scaled = (
        lax.all_to_all(send_x, "group", split_axis=0, concat_axis=0, tiled=True),
        lax.all_to_all(send_scaled, "group", split_axis=0, concat_axis=0, tiled=True),
    )
    grad_gate, grad_up, grad_down, partial_rows = slice_backward(
        rows_x.reshape(block_rows, features),
        rows_scaled.reshape(block_rows, features),
        w_gate[0],
        w_up[0],
        w_down[0],
    )
    returned = lax.all_to_all(
        partial_rows.reshape(groups, capacity, features),
        "group",
        split_axis=0,
        concat_axis=0,
        tiled=True,
    )
    returned = returned.reshape(block_rows, features)
    row_numbers = jnp.arange(tokens.shape[0] * lax.axis_size("member"), dtype=jnp.int32)
    selector = (row_numbers[:, None] == flat_slots[None, :]).astype(jnp.float32)
    summed = lax.psum_scatter(
        jnp.dot(
            selector, returned, precision=lax.Precision.HIGHEST, preferred_element_type=jnp.float32
        ),
        "member",
        scatter_dimension=0,
        tiled=True,
    )
    return (summed.astype(jnp.bfloat16), grad_gate[None], grad_up[None], grad_down[None])


def shards(tokens, grad_out, route_token, *rest):
    devices = lax.axis_size("group") * lax.axis_size("member")
    _, groups, experts, capacity = route_token.shape
    dense = devices * tokens.shape[0] <= groups * capacity and experts == 1
    paired = tokens.shape[0] == 1 and devices & (devices - 1) == 0
    body = dense_shards if dense and paired else routed_shards
    return body(tokens, grad_out, route_token, *rest)


def solution(mesh):
    placed = (
        P(("group", "member"), None),
        P(("group", "member"), None),
        P("group", None, None, None),
        P("group", None, None),
        P("group", None, None, None),
        P(("group", "member"), None, None),
        P(("group", "member"), None, None),
        P(("group", "member"), None, None),
    )
    return jax.shard_map(
        shards,
        mesh=mesh,
        in_specs=placed,
        out_specs=(
            P(("group", "member"), None),
            P(("group", "member"), None, None),
            P(("group", "member"), None, None),
            P(("group", "member"), None, None),
        ),
        check_vma=False,
    )
```

profile of v0, /device:TPU:0, one launch (start us, length us, event | category | flops | bytes accessed | tf_op | source)
XLA Modules:
  0.0 36.1 jit_solution(6255586348713922829)
XLA Ops:
  0.6 0.0 copy-start
  0.6 0.0 copy-start.1
  0.7 0.0 copy-start.2
  0.7 1.0 %pack_rows.1 = bf16[16,56,128]{2,1,0:T(8,128)(2,1)S(1)} custom-call(bf16[1,3584]{1,0:T(2,128)(2,1)} %tokens_hbm.1, bf16[1,3584]{1,0:T(2,128)(2,1)} %grad_hbm.1, s32[1,4,1,8]{3,2,1,0:T(1,128)} %token_hbm.1, s32[1,1,4]{2,1,0:T(1,128)} %bitcast.2, f32[1,4,1,8]{3,2,1,0:T(1,128)} %prob_hbm.1), custom_call_target="tpu_custom_call" | custom-call | flops 18350080000 | bytes 7340032 | tf_op jit(solution)/shard_map/pack_rows/pallas_call | solution.py:177
  1.7 17.4 %all_to_all.10.mine_ref = bf16[16,56,128]{2,1,0:T(8,128)(2,1)S(1)} all-to-all(bf16[16,56,128]{2,1,0:T(8,128)(2,1)S(1)} %pack_rows.1), channel_id=1, replica_groups={{0,2,4,6,8,10,12,14,16,18,20,22,24,26,28,30},{1,3,5,7,9,11,13,15,17,19,..., dimensions={0} | all-to-all | bytes 458752 | tf_op jit(solution)/shard_map/all_to_all | solution.py:202
  19.0 0.0 collective-permute-start
  19.0 0.1 unpack_rows.1.mine_ref
  19.2 1.4 %collective-permute-done.other_ref = bf16[16,56,128]{2,1,0:T(8,128)(2,1)S(1)} collective-permute-done((bf16[16,56,128]{2,1,0:T(8,128)(2,1)S(1)}, bf16[16,56,128]{2,1,0:T(8,128)(2,1)S(1)}, u32[]{:S(2)}, u32[]{:S(2)}) %collective-permute-start) | collective-permute-done | bytes 229408 | tf_op jit(solution)/shard_map/ppermute | solution.py:161
  20.5 0.0 copy-done
  20.5 0.0 copy-done.1
  20.5 0.0 copy-done.2
  20.5 2.5 %partial_rows.1 = (bf16[16,2,7,4,128]{4,3,2,1,0:T(4,128)(2,1)}, bf16[32,7168]{1,0:T(8,128)(2,1)S(1)}, bf16[384,32]{1,0:T(8,128)(2,1)S(1)}) custom-call(bf16[16,7168]{1,0:T(8,128)(2,1)S(1)} %unpack_rows.1.mine_ref, bf16[16,56,128]{2,1,0:T(8,128)(2,1)S(1)} %collective-permute-done.other_ref, bf16[1,128,3584]{2,1,0:T(8,128)(2,1)S(1)} %copy-done, ...), custom_call_target="tpu_custom_call" | custom-call | tf_op jit(solution)/shard_map/partial_rows/pallas_call | solution.py:214
  23.0 2.6 %all-to-all-start.1 = ((bf16[32,7,4,128]{3,2,1,0:T(4,128)(2,1)}), bf16[32,7,4,128]{3,2,1,0:T(4,128)(2,1)S(1)}, u32[]{:S(2)}, u32[]{:S(2)}) async-start(bf16[32,7,4,128]{3,2,1,0:T(4,128)(2,1)} %bitcast.1), calls=%async_computation.1 | async-start | bytes 458752 | tf_op jit(solution)/shard_map/all_to_all | solution.py:245
  25.6 1.8 %weight_grads.1 = (bf16[1,128,3584]{2,1,0:T(8,128)(2,1)}, bf16[1,128,3584]{2,1,0:T(8,128)(2,1)}, bf16[1,128,3584]{2,1,0:T(8,128)(2,1)}) custom-call(bf16[32,7168]{1,0:T(8,128)(2,1)S(1)} %get-tuple-element.11.rows_ref, bf16[384,32]{1,0:T(8,128)(2,1)S(1)} %get-tuple-element.12.acts_ref), custom_call_target="tpu_custom_call" | custom-call | flops 88080384 | bytes 2752512 | tf_op jit(solution)/shard_map/weight_grads/pallas_call | solution.py:228
  27.5 8.0 %all-to-all-done.1.back_ref = bf16[32,7,4,128]{3,2,1,0:T(4,128)(2,1)S(1)} async-done(((bf16[32,7,4,128]{3,2,1,0:T(4,128)(2,1)}), bf16[32,7,4,128]{3,2,1,0:T(4,128)(2,1)S(1)}, u32[]{:S(2)}, u32[]{:S(2)}) %all-to-all-start.1) | async-done | bytes 229408 | tf_op jit(solution)/shard_map/all_to_all | solution.py:245
  35.4 0.7 %sum_rows.1 = bf16[1,3584]{1,0:T(2,128)(2,1)} custom-call(bf16[32,7,4,128]{3,2,1,0:T(4,128)(2,1)S(1)} %all-to-all-done.1.back_ref), custom_call_target="tpu_custom_call" | custom-call | tf_op jit(solution)/shard_map/sum_rows/pallas_call | solution.py:248
Async XLA Ops:
  0.6 19.9 %copy-start = (bf16[1,128,3584]{2,1,0:T(8,128)(2,1)S(1)}, bf16[1,128,3584]{2,1,0:T(8,128)(2,1)}, u32[]{:S(2)}) copy-start(bf16[1,128,3584]{2,1,0:T(8,128)(2,1)} %gate_ref.1) | copy-start | bytes 2752516
  0.6 19.9 %copy-start.1 = (bf16[1,128,3584]{2,1,0:T(8,128)(2,1)S(1)}, bf16[1,128,3584]{2,1,0:T(8,128)(2,1)}, u32[]{:S(2)}) copy-start(bf16[1,128,3584]{2,1,0:T(8,128)(2,1)} %up_ref.1) | copy-start | bytes 2752516
  0.7 19.9 %copy-start.2 = (bf16[1,128,3584]{2,1,0:T(8,128)(2,1)S(1)}, bf16[1,128,3584]{2,1,0:T(8,128)(2,1)}, u32[]{:S(2)}) copy-start(bf16[1,128,3584]{2,1,0:T(8,128)(2,1)} %down_ref.1) | copy-start | bytes 2752516
  19.0 1.5 %collective-permute-start = (bf16[16,56,128]{2,1,0:T(8,128)(2,1)S(1)}, bf16[16,56,128]{2,1,0:T(8,128)(2,1)S(1)}, u32[]{:S(2)}, u32[]{:S(2)}) collective-permute-start(bf16[16,56,128]{2,1,0:T(8,128)(2,1)S(1)} %all_to_all.10.mine_ref), channel_id=1, source_target_pairs={{0,1},{1,0},{2,3},{3,2},{4,5},{5,4},{6,7},{7,6},{8,9},{9,8},{10,11... | collective-permute-start | bytes 688136 | tf_op jit(solution)/shard_map/ppermute | solution.py:161
  23.0 12.4 %all-to-all-start.1 = ((bf16[32,7,4,128]{3,2,1,0:T(4,128)(2,1)}), bf16[32,7,4,128]{3,2,1,0:T(4,128)(2,1)S(1)}, u32[]{:S(2)}, u32[]{:S(2)}) async-start(bf16[32,7,4,128]{3,2,1,0:T(4,128)(2,1)} %bitcast.1), calls=%async_computation.1 | async-start | bytes 458752 | tf_op jit(solution)/shard_map/all_to_all | solution.py:245
where the time goes:
time: 36.4 us; the launch traced here: 36.1 us
  blocking collectives  17.4 us (48%)
  waiting for transfers between devices  9.34 us (26%)
  Pallas kernels  6.13 us (17%)
  starting transfers between devices  2.58 us (7%)
  between operations  0.69 us (2%)
    all_to_all x1, blocking collectives, dense_shards(): mine = trade(copies)  17.4 us
    all_to_all x1, waiting for transfers between devices, dense_shards(): lax.all_to_all(sent.reshape(count, chunks // 4, 4, LANES), AXES, 0, 0, ti...  7.98 us
    all_to_all x1, starting transfers between devices, dense_shards(): lax.all_to_all(sent.reshape(count, chunks // 4, 4, LANES), AXES, 0, 0, ti...  2.58 us
    pallas_call x1, Pallas kernels, dense_shards(): pl.pallas_call(functools.partial(partial_kernel, chunks), out_shape=(jax....  2.48 us
    pallas_call x1, Pallas kernels, dense_shards(): pl.pallas_call(functools.partial(grads_kernel, features), out_shape=(grad...  1.83 us
    ppermute x1, waiting for transfers between devices, exchange(): return lax.ppermute(value, AXES, [(i, i ^ distance) for i in range(count)])  1.36 us
    pallas_call x1, Pallas kernels, dense_shards(): pl.pallas_call(functools.partial(pack_kernel, chunks), out_shape=pltpu.VM...  1 us
  transfers between devices with their start and end apart: 2, of which 2 were waited for; matrix products, arithmetic and copies ran while one was open for 0% of the time, Pallas kernels for 5%

commit v1 on v0

--- a/solution.py
+++ b/solution.py
@@ -66,48 +66,46 @@
             out_ref[g * places + n] = packed
 
 
-def unpack_rows(chunks, packed_ref, wide_ref, rows_ref):
+def unpack_kernel(chunks, packed_ref, x_ref, scaled_ref, wide_ref):
     tokens, rows, _ = packed_ref.shape
     wide_ref[...] = packed_ref[...].astype(jnp.float32).reshape(tokens * rows, LANES)
-    for k in range(rows):
-        column = wide_ref[pl.ds(k, tokens, stride=rows), :]
-        rows_ref[:, k * LANES : (k + 1) * LANES] = column.astype(jnp.bfloat16)
-
-
-def unpack_kernel(chunks, mine_ref, rows_ref, wide_ref):
-    unpack_rows(chunks, mine_ref, wide_ref, rows_ref)
+    for n, out_ref in enumerate((x_ref, scaled_ref)):
+        for k in range(chunks):
+            column = wide_ref[pl.ds(n * chunks + k, tokens, stride=rows), :]
+            out_ref[:, k * LANES : (k + 1) * LANES] = column.astype(jnp.bfloat16)
+
+
+def first_kernel(mine_ref, other_ref, gate_ref, up_ref, values_ref):
+    x = jnp.concatenate([mine_ref[...], other_ref[...]], axis=0)
+    both = jnp.concatenate([gate_ref[0], up_ref[0]], axis=0)
+    values_ref[...] = lax.dot_general(both, x, NT, preferred_element_type=jnp.float32)
 
 
 def partial_kernel(
     chunks,
+    values_ref,
     mine_ref,
     other_ref,
     gate_ref,
     up_ref,
     down_ref,
     sent_ref,
-    rows_ref,
     acts_ref,
-    wide_ref,
     spread_ref,
 ):
     count = mine_ref.shape[0]
     tokens = 2 * count
-    features = chunks * LANES
     units = gate_ref.shape[1]
-    rows_ref[:count] = mine_ref[...]
-    unpack_rows(chunks, other_ref, wide_ref, rows_ref.at[pl.ds(count, count)])
-    x, scaled = rows_ref[:, :features], rows_ref[:, features:]
-    both = jnp.concatenate([gate_ref[0], up_ref[0]], axis=0)
-    values = lax.dot_general(both, x, NT, preferred_element_type=jnp.float32)
-    gate_value, up_value = values[:units], values[units:]
+    scaled = jnp.concatenate([mine_ref[...], other_ref[...]], axis=0)
     d_hidden = lax.dot_general(down_ref[0], scaled, NT, preferred_element_type=jnp.float32)
+    gate_value, up_value = values_ref[:units], values_ref[units:]
     sigma_gate = jax.nn.sigmoid(gate_value)
     active = gate_value * sigma_gate
     d_gate = d_hidden * up_value * sigma_gate * (1.0 + gate_value * (1.0 - sigma_gate))
     acts_ref[0:units] = d_gate.astype(jnp.bfloat16)
     acts_ref[units : 2 * units] = (d_hidden * active).astype(jnp.bfloat16)
     acts_ref[2 * units :] = (active * up_value).astype(jnp.bfloat16)
+    both = jnp.concatenate([gate_ref[0], up_ref[0]], axis=0)
     partial = lax.dot_general(
         acts_ref[: 2 * units], both, TN, preferred_element_type=jnp.float32
     )
@@ -124,13 +122,23 @@
 
 
 def grads_kernel(
-    features, rows_ref, acts_ref, gate_out, up_out, down_out, held_ref, sems
+    mine_x_ref,
+    other_x_ref,
+    mine_scaled_ref,
+    other_scaled_ref,
+    acts_ref,
+    gate_out,
+    up_out,
+    down_out,
+    held_ref,
+    sems,
 ):
     units = held_ref.shape[1]
     height = units // PARTS
+    x = jnp.concatenate([mine_x_ref[...], other_x_ref[...]], axis=0)
+    scaled = jnp.concatenate([mine_scaled_ref[...], other_scaled_ref[...]], axis=0)
     copies = []
-    for n, (out, first) in enumerate(((gate_out, 0), (up_out, 0), (down_out, features))):
-        right = rows_ref[:, first : first + features]
+    for n, (out, right) in enumerate(((gate_out, x), (up_out, x), (down_out, scaled))):
         for k in range(PARTS):
             left = acts_ref[n * units + k * height : n * units + (k + 1) * height, :]
             held_ref[n, k * height : (k + 1) * height] = jnp.dot(
@@ -200,35 +208,43 @@
         axis_index_groups=cores,
     )
     mine = trade(copies)
-    other = exchange(mine, 1)
-    wide = pltpu.VMEM((half * rows, LANES), jnp.float32)
-    unpacked = pl.pallas_call(
+    half_rows = pltpu.VMEM((half, features), jnp.bfloat16)
+    mine_x, mine_scaled = pl.pallas_call(
         functools.partial(unpack_kernel, chunks),
-        out_shape=pltpu.VMEM((half, 2 * features), jnp.bfloat16),
+        out_shape=(half_rows,) * 2,
         in_specs=[VMEM],
-        out_specs=VMEM,
-        scratch_shapes=[wide],
+        out_specs=(VMEM,) * 2,
+        scratch_shapes=[pltpu.VMEM((half * rows, LANES), jnp.float32)],
         compiler_params=pltpu.CompilerParams(vmem_limit_bytes=2 * 1024 * 1024),
         name="unpack_rows",
     )(mine)
-    sent, both, acts = pl.pallas_call(
+    other_x = exchange(mine_x, 1)
+    other_scaled = exchange(mine_scaled, 1)
+    values = pl.pallas_call(
+        first_kernel,
+        out_shape=pltpu.VMEM((2 * units, count), jnp.float32),
+        in_specs=[VMEM] * 4,
+        out_specs=VMEM,
+        compiler_params=pltpu.CompilerParams(vmem_limit_bytes=8 * 1024 * 1024),
+        name="gate_up",
+    )(mine_x, other_x, w_gate, w_up)
+    sent, acts = pl.pallas_call(
         functools.partial(partial_kernel, chunks),
         out_shape=(
             jax.ShapeDtypeStruct((half, 2, chunks // 4, 4, LANES), jnp.bfloat16),
-            pltpu.VMEM((count, 2 * features), jnp.bfloat16),
             pltpu.VMEM((3 * units, count), jnp.bfloat16),
         ),
-        in_specs=[VMEM] * 5,
-        out_specs=(VMEM,) * 3,
-        scratch_shapes=[wide, pltpu.VMEM((count * chunks, LANES), jnp.float32)],
+        in_specs=[VMEM] * 6,
+        out_specs=(VMEM,) * 2,
+        scratch_shapes=[pltpu.VMEM((count * chunks, LANES), jnp.float32)],
         compiler_params=pltpu.CompilerParams(vmem_limit_bytes=16 * 1024 * 1024),
         name="partial_rows",
-    )(unpacked, other, w_gate, w_up, w_down)
+    )(values, mine_scaled, other_scaled, w_gate, w_up, w_down)
     grad_shape = jax.ShapeDtypeStruct((1, units, features), jnp.bfloat16)
     grad_gate, grad_up, grad_down = pl.pallas_call(
-        functools.partial(grads_kernel, features),
+        grads_kernel,
         out_shape=(grad_shape,) * 3,
-        in_specs=[VMEM] * 2,
+        in_specs=[VMEM] * 5,
         out_specs=(HBM, HBM, HBM),
         scratch_shapes=[
             pltpu.VMEM((3, units, features), jnp.bfloat16),
@@ -241,7 +257,7 @@
             transcendentals=0,
         ),
         name="weight_grads",
-    )(both, acts)
+    )(mine_x, other_x, mine_scaled, other_scaled, acts)
     back = lax.all_to_all(
         sent.reshape(count, chunks // 4, 4, LANES), AXES, 0, 0, tiled=True
     )

time: 36.4 us -> 36.5 us (level)
  starting transfers between devices: 2.58 us -> 3.14 us
  waiting for transfers between devices: 9.34 us -> 8.81 us
    pallas_call x2 -> x3, Pallas kernels: 1.95 us -> 2.54 us  [the longest x1 1.82 us: dense_shards(): pl.pallas_call(grads_kernel, out_shape=(grad_shape,) * 3, in_specs=[VMEM]...]
    ppermute x1 -> x2, starting transfers between devices: 0.01 us -> 0.56 us  [exchange(): return lax.ppermute(value, AXES, [(i, i ^ distance) for i in range(count)])]
    ppermute x1 -> x2, waiting for transfers between devices: 1.36 us -> 0.81 us  [exchange(): return lax.ppermute(value, AXES, [(i, i ^ distance) for i in range(count)])]
    pallas_call x1, Pallas kernels: 2.48 us -> 1.95 us  [dense_shards(): pl.pallas_call(functools.partial(partial_kernel, chunks), out_shape=(jax....]
  transfers between devices with their start and end apart: 2 -> 3, of which waited for: 2 -> 2; matrix products, arithmetic and copies ran while one was open for 0% -> 0% of each run, Pallas kernels for 5% -> 7%
where the time goes in v1:
time: 36.5 us; the launch traced here: 36.2 us
  blocking collectives  17.4 us (48%)
  waiting for transfers between devices  8.81 us (24%)
  Pallas kernels  6.17 us (17%)
  starting transfers between devices  3.14 us (9%)
  between operations  0.72 us (2%)
    all_to_all x1, blocking collectives, dense_shards(): mine = trade(copies)  17.4 us
    all_to_all x1, waiting for transfers between devices, dense_shards(): lax.all_to_all(sent.reshape(count, chunks // 4, 4, LANES), AXES, 0, 0, ti...  7.99 us
    all_to_all x1, starting transfers between devices, dense_shards(): lax.all_to_all(sent.reshape(count, chunks // 4, 4, LANES), AXES, 0, 0, ti...  2.58 us
    pallas_call x1, Pallas kernels, dense_shards(): pl.pallas_call(functools.partial(partial_kernel, chunks), out_shape=(jax....  1.95 us
    pallas_call x1, Pallas kernels, dense_shards(): pl.pallas_call(grads_kernel, out_shape=(grad_shape,) * 3, in_specs=[VMEM]...  1.82 us
    pallas_call x1, Pallas kernels, dense_shards(): pl.pallas_call(functools.partial(pack_kernel, chunks), out_shape=pltpu.VM...  0.99 us
    ppermute x2, waiting for transfers between devices, exchange(): return lax.ppermute(value, AXES, [(i, i ^ distance) for i in range(count)])  0.81 us
  transfers between devices with their start and end apart: 3, of which 2 were waited for; matrix products, arithmetic and copies ran while one was open for 0% of the time, Pallas kernels for 7%

profile of v1, /device:TPU:0, one launch (start us, length us, event | category | flops | bytes accessed | tf_op | source)
XLA Modules:
  0.0 36.2 jit_solution(4885412259248819314)
XLA Ops:
  0.6 0.0 copy-start
  0.6 0.0 copy-start.1
  0.7 1.0 %pack_rows.1 = bf16[16,56,128]{2,1,0:T(8,128)(2,1)S(1)} custom-call(bf16[1,3584]{1,0:T(2,128)(2,1)} %tokens_hbm.1, bf16[1,3584]{1,0:T(2,128)(2,1)} %grad_hbm.1, s32[1,4,1,8]{3,2,1,0:T(1,128)} %token_hbm.1, s32[1,1,4]{2,1,0:T(1,128)} %bitcast.2, f32[1,4,1,8]{3,2,1,0:T(1,128)} %prob_hbm.1), custom_call_target="tpu_custom_call" | custom-call | flops 18350080000 | bytes 7340032 | tf_op jit(solution)/shard_map/pack_rows/pallas_call | solution.py:185
  1.6 17.4 %all_to_all.10.packed_ref = bf16[16,56,128]{2,1,0:T(8,128)(2,1)S(1)} all-to-all(bf16[16,56,128]{2,1,0:T(8,128)(2,1)S(1)} %pack_rows.1), channel_id=1, replica_groups={{0,2,4,6,8,10,12,14,16,18,20,22,24,26,28,30},{1,3,5,7,9,11,13,15,17,19,..., dimensions={0} | all-to-all | bytes 458752 | tf_op jit(solution)/shard_map/all_to_all | solution.py:210
  19.0 0.1 unpack_rows.1
  19.1 0.1 collective-permute-start
  19.2 0.0 copy-start.2
  19.2 0.5 %collective-permute-start.1 = (bf16[16,3584]{1,0:T(8,128)(2,1)S(1)}, bf16[16,3584]{1,0:T(8,128)(2,1)S(1)}, u32[]{:S(2)}, u32[]{:S(2)}) collective-permute-start(bf16[16,3584]{1,0:T(8,128)(2,1)S(1)} %get-tuple-element.12.mine_ref.mine_scaled_ref), channel_id=1, source_target_pairs={{0,1},{1,0},{2,3},{3,2},{4,5},{5,4},{6,7},{7,6},{8,9},{9,8},{10,11... | collective-permute-start | bytes 344072 | tf_op jit(solution)/shard_map/ppermute | solution.py:169
  19.7 0.8 %collective-permute-done.other_ref.other_x_ref = bf16[16,3584]{1,0:T(8,128)(2,1)S(1)} collective-permute-done((bf16[16,3584]{1,0:T(8,128)(2,1)S(1)}, bf16[16,3584]{1,0:T(8,128)(2,1)S(1)}, u32[]{:S(2)}, u32[]{:S(2)}) %collective-permute-start) | collective-permute-done | bytes 114720 | tf_op jit(solution)/shard_map/ppermute | solution.py:169
  20.5 0.0 copy-done
  20.5 0.0 copy-done.1
  20.5 0.6 %gate_up.1.values_ref = f32[256,32]{1,0:T(8,128)S(1)} custom-call(bf16[16,3584]{1,0:T(8,128)(2,1)S(1)} %get-tuple-element.11.mine_ref.mine_x_ref, bf16[16,3584]{1,0:T(8,128)(2,1)S(1)} %collective-permute-done.other_ref.other_x_ref, bf16[1,128,3584]{2,1,0:T(8,128)(2,1)S(1)} %copy-done, bf16[1,128,3584]{2,1,0:T(8,128)(2,1)S(1)} %copy-done.1), custom_call_target="tpu_custom_call" | custom-call | tf_op jit(solution)/shard_map/gate_up/pallas_call | solution.py:223
  21.1 0.0 collective-permute-done.1.other_ref.other_scaled_ref
  21.2 0.0 copy-done.2
  21.2 2.0 %partial_rows.1 = (bf16[16,2,7,4,128]{4,3,2,1,0:T(4,128)(2,1)}, bf16[384,32]{1,0:T(8,128)(2,1)S(1)}) custom-call(f32[256,32]{1,0:T(8,128)S(1)} %gate_up.1.values_ref, bf16[16,3584]{1,0:T(8,128)(2,1)S(1)} %get-tuple-element.12.mine_ref.mine_scaled_ref, bf16[16,3584]{1,0:T(8,128)(2,1)S(1)} %collective-permute-done.1.other_ref.other_scaled_ref, ...), custom_call_target="tpu_custom_call" | custom-call | tf_op jit(solution)/shard_map/partial_rows/pallas_call | solution.py:231
  23.1 2.6 %all-to-all-start.1 = ((bf16[32,7,4,128]{3,2,1,0:T(4,128)(2,1)}), bf16[32,7,4,128]{3,2,1,0:T(4,128)(2,1)S(1)}, u32[]{:S(2)}, u32[]{:S(2)}) async-start(bf16[32,7,4,128]{3,2,1,0:T(4,128)(2,1)} %bitcast.1), calls=%async_computation.1 | async-start | bytes 458752 | tf_op jit(solution)/shard_map/all_to_all | solution.py:261
  25.7 1.8 %weight_grads.1 = (bf16[1,128,3584]{2,1,0:T(8,128)(2,1)}, bf16[1,128,3584]{2,1,0:T(8,128)(2,1)}, bf16[1,128,3584]{2,1,0:T(8,128)(2,1)}) custom-call(bf16[16,3584]{1,0:T(8,128)(2,1)S(1)} %get-tuple-element.11.mine_ref.mine_x_ref, bf16[16,3584]{1,0:T(8,128)(2,1)S(1)} %collective-permute-done.other_ref.other_x_ref, ...), custom_call_target="tpu_custom_call" | custom-call | flops 88080384 | bytes 2752512 | tf_op jit(solution)/shard_map/weight_grads/pallas_call | solution.py:244
  27.5 8.0 %all-to-all-done.1.back_ref = bf16[32,7,4,128]{3,2,1,0:T(4,128)(2,1)S(1)} async-done(((bf16[32,7,4,128]{3,2,1,0:T(4,128)(2,1)}), bf16[32,7,4,128]{3,2,1,0:T(4,128)(2,1)S(1)}, u32[]{:S(2)}, u32[]{:S(2)}) %all-to-all-start.1) | async-done | bytes 229408 | tf_op jit(solution)/shard_map/all_to_all | solution.py:261
  35.5 0.7 %sum_rows.1 = bf16[1,3584]{1,0:T(2,128)(2,1)} custom-call(bf16[32,7,4,128]{3,2,1,0:T(4,128)(2,1)S(1)} %all-to-all-done.1.back_ref), custom_call_target="tpu_custom_call" | custom-call | tf_op jit(solution)/shard_map/sum_rows/pallas_call | solution.py:264
Async XLA Ops:
  0.6 19.9 %copy-start = (bf16[1,128,3584]{2,1,0:T(8,128)(2,1)S(1)}, bf16[1,128,3584]{2,1,0:T(8,128)(2,1)}, u32[]{:S(2)}) copy-start(bf16[1,128,3584]{2,1,0:T(8,128)(2,1)} %gate_ref.3) | copy-start | bytes 2752516
  0.6 19.9 %copy-start.1 = (bf16[1,128,3584]{2,1,0:T(8,128)(2,1)S(1)}, bf16[1,128,3584]{2,1,0:T(8,128)(2,1)}, u32[]{:S(2)}) copy-start(bf16[1,128,3584]{2,1,0:T(8,128)(2,1)} %up_ref.3) | copy-start | bytes 2752516
  19.1 1.4 %collective-permute-start = (bf16[16,3584]{1,0:T(8,128)(2,1)S(1)}, bf16[16,3584]{1,0:T(8,128)(2,1)S(1)}, u32[]{:S(2)}, u32[]{:S(2)}) collective-permute-start(bf16[16,3584]{1,0:T(8,128)(2,1)S(1)} %get-tuple-element.11.mine_ref.mine_x_ref), channel_id=1, source_target_pairs={{0,1},{1,0},{2,3},{3,2},{4,5},{5,4},{6,7},{7,6},{8,9},{9,8},{10,11... | collective-permute-start | bytes 344072 | tf_op jit(solution)/shard_map/ppermute | solution.py:169
  19.2 1.9 %copy-start.2 = (bf16[1,128,3584]{2,1,0:T(8,128)(2,1)S(1)}, bf16[1,128,3584]{2,1,0:T(8,128)(2,1)}, u32[]{:S(2)}) copy-start(bf16[1,128,3584]{2,1,0:T(8,128)(2,1)} %down_ref.1) | copy-start | bytes 2752516
  19.2 1.9 %collective-permute-start.1 = (bf16[16,3584]{1,0:T(8,128)(2,1)S(1)}, bf16[16,3584]{1,0:T(8,128)(2,1)S(1)}, u32[]{:S(2)}, u32[]{:S(2)}) collective-permute-start(bf16[16,3584]{1,0:T(8,128)(2,1)S(1)} %get-tuple-element.12.mine_ref.mine_scaled_ref), channel_id=1, source_target_pairs={{0,1},{1,0},{2,3},{3,2},{4,5},{5,4},{6,7},{7,6},{8,9},{9,8},{10,11... | collective-permute-start | bytes 344072 | tf_op jit(solution)/shard_map/ppermute | solution.py:169
  23.1 12.4 %all-to-all-start.1 = ((bf16[32,7,4,128]{3,2,1,0:T(4,128)(2,1)}), bf16[32,7,4,128]{3,2,1,0:T(4,128)(2,1)S(1)}, u32[]{:S(2)}, u32[]{:S(2)}) async-start(bf16[32,7,4,128]{3,2,1,0:T(4,128)(2,1)} %bitcast.1), calls=%async_computation.1 | async-start | bytes 458752 | tf_op jit(solution)/shard_map/all_to_all | solution.py:261

commit v2 on v0

--- a/solution.py
+++ b/solution.py
@@ -214,7 +214,7 @@
     sent, both, acts = pl.pallas_call(
         functools.partial(partial_kernel, chunks),
         out_shape=(
-            jax.ShapeDtypeStruct((half, 2, chunks // 4, 4, LANES), jnp.bfloat16),
+            pltpu.VMEM((half, 2, chunks // 4, 4, LANES), jnp.bfloat16),
             pltpu.VMEM((count, 2 * features), jnp.bfloat16),
             pltpu.VMEM((3 * units, count), jnp.bfloat16),
         ),

time: 36.4 us -> 36.4 us (level)
  no operation moved by 1% of the time
where the time goes in v2:
time: 36.4 us; the launch traced here: 36.1 us
  blocking collectives  17.4 us (48%)
  waiting for transfers between devices  9.34 us (26%)
  Pallas kernels  6.13 us (17%)
  starting transfers between devices  2.58 us (7%)
  between operations  0.69 us (2%)
    all_to_all x1, blocking collectives, dense_shards(): mine = trade(copies)  17.4 us
    all_to_all x1, waiting for transfers between devices, dense_shards(): lax.all_to_all(sent.reshape(count, chunks // 4, 4, LANES), AXES, 0, 0, ti...  7.98 us
    all_to_all x1, starting transfers between devices, dense_shards(): lax.all_to_all(sent.reshape(count, chunks // 4, 4, LANES), AXES, 0, 0, ti...  2.58 us
    pallas_call x1, Pallas kernels, dense_shards(): pl.pallas_call(functools.partial(partial_kernel, chunks), out_shape=(pltp...  2.48 us
    pallas_call x1, Pallas kernels, dense_shards(): pl.pallas_call(functools.partial(grads_kernel, features), out_shape=(grad...  1.83 us
    ppermute x1, waiting for transfers between devices, exchange(): return lax.ppermute(value, AXES, [(i, i ^ distance) for i in range(count)])  1.36 us
    pallas_call x1, Pallas kernels, dense_shards(): pl.pallas_call(functools.partial(pack_kernel, chunks), out_shape=pltpu.VM...  1 us
  transfers between devices with their start and end apart: 2, of which 2 were waited for; matrix products, arithmetic and copies ran while one was open for 0% of the time, Pallas kernels for 5%

profile of v2, /device:TPU:0, one launch (start us, length us, event | category | flops | bytes accessed | tf_op | source)
XLA Modules:
  0.0 36.1 jit_solution(6255586348713922829)
XLA Ops:
  0.6 0.0 copy-start
  0.6 0.0 copy-start.1
  0.7 0.0 copy-start.2
  0.7 1.0 %pack_rows.1 = bf16[16,56,128]{2,1,0:T(8,128)(2,1)S(1)} custom-call(bf16[1,3584]{1,0:T(2,128)(2,1)} %tokens_hbm.1, bf16[1,3584]{1,0:T(2,128)(2,1)} %grad_hbm.1, s32[1,4,1,8]{3,2,1,0:T(1,128)} %token_hbm.1, s32[1,1,4]{2,1,0:T(1,128)} %bitcast.2, f32[1,4,1,8]{3,2,1,0:T(1,128)} %prob_hbm.1), custom_call_target="tpu_custom_call" | custom-call | flops 18350080000 | bytes 7340032 | tf_op jit(solution)/shard_map/pack_rows/pallas_call | solution.py:177
  1.7 17.4 %all_to_all.10.mine_ref = bf16[16,56,128]{2,1,0:T(8,128)(2,1)S(1)} all-to-all(bf16[16,56,128]{2,1,0:T(8,128)(2,1)S(1)} %pack_rows.1), channel_id=1, replica_groups={{0,2,4,6,8,10,12,14,16,18,20,22,24,26,28,30},{1,3,5,7,9,11,13,15,17,19,..., dimensions={0} | all-to-all | bytes 458752 | tf_op jit(solution)/shard_map/all_to_all | solution.py:202
  19.0 0.0 collective-permute-start
  19.0 0.1 unpack_rows.1.mine_ref
  19.2 1.4 %collective-permute-done.other_ref = bf16[16,56,128]{2,1,0:T(8,128)(2,1)S(1)} collective-permute-done((bf16[16,56,128]{2,1,0:T(8,128)(2,1)S(1)}, bf16[16,56,128]{2,1,0:T(8,128)(2,1)S(1)}, u32[]{:S(2)}, u32[]{:S(2)}) %collective-permute-start) | collective-permute-done | bytes 229408 | tf_op jit(solution)/shard_map/ppermute | solution.py:161
  20.5 0.0 copy-done
  20.5 0.0 copy-done.1
  20.5 0.0 copy-done.2
  20.5 2.5 %partial_rows.1 = (bf16[16,2,7,4,128]{4,3,2,1,0:T(4,128)(2,1)}, bf16[32,7168]{1,0:T(8,128)(2,1)S(1)}, bf16[384,32]{1,0:T(8,128)(2,1)S(1)}) custom-call(bf16[16,7168]{1,0:T(8,128)(2,1)S(1)} %unpack_rows.1.mine_ref, bf16[16,56,128]{2,1,0:T(8,128)(2,1)S(1)} %collective-permute-done.other_ref, bf16[1,128,3584]{2,1,0:T(8,128)(2,1)S(1)} %copy-done, ...), custom_call_target="tpu_custom_call" | custom-call | tf_op jit(solution)/shard_map/partial_rows/pallas_call | solution.py:214
  23.0 2.6 %all-to-all-start.1 = ((bf16[32,7,4,128]{3,2,1,0:T(4,128)(2,1)}), bf16[32,7,4,128]{3,2,1,0:T(4,128)(2,1)S(1)}, u32[]{:S(2)}, u32[]{:S(2)}) async-start(bf16[32,7,4,128]{3,2,1,0:T(4,128)(2,1)} %bitcast.1), calls=%async_computation.1 | async-start | bytes 458752 | tf_op jit(solution)/shard_map/all_to_all | solution.py:245
  25.6 1.8 %weight_grads.1 = (bf16[1,128,3584]{2,1,0:T(8,128)(2,1)}, bf16[1,128,3584]{2,1,0:T(8,128)(2,1)}, bf16[1,128,3584]{2,1,0:T(8,128)(2,1)}) custom-call(bf16[32,7168]{1,0:T(8,128)(2,1)S(1)} %get-tuple-element.11.rows_ref, bf16[384,32]{1,0:T(8,128)(2,1)S(1)} %get-tuple-element.12.acts_ref), custom_call_target="tpu_custom_call" | custom-call | flops 88080384 | bytes 2752512 | tf_op jit(solution)/shard_map/weight_grads/pallas_call | solution.py:228
  27.5 8.0 %all-to-all-done.1.back_ref = bf16[32,7,4,128]{3,2,1,0:T(4,128)(2,1)S(1)} async-done(((bf16[32,7,4,128]{3,2,1,0:T(4,128)(2,1)}), bf16[32,7,4,128]{3,2,1,0:T(4,128)(2,1)S(1)}, u32[]{:S(2)}, u32[]{:S(2)}) %all-to-all-start.1) | async-done | bytes 229408 | tf_op jit(solution)/shard_map/all_to_all | solution.py:245
  35.4 0.7 %sum_rows.1 = bf16[1,3584]{1,0:T(2,128)(2,1)} custom-call(bf16[32,7,4,128]{3,2,1,0:T(4,128)(2,1)S(1)} %all-to-all-done.1.back_ref), custom_call_target="tpu_custom_call" | custom-call | tf_op jit(solution)/shard_map/sum_rows/pallas_call | solution.py:248
Async XLA Ops:
  0.6 19.9 %copy-start = (bf16[1,128,3584]{2,1,0:T(8,128)(2,1)S(1)}, bf16[1,128,3584]{2,1,0:T(8,128)(2,1)}, u32[]{:S(2)}) copy-start(bf16[1,128,3584]{2,1,0:T(8,128)(2,1)} %gate_ref.1) | copy-start | bytes 2752516
  0.6 19.9 %copy-start.1 = (bf16[1,128,3584]{2,1,0:T(8,128)(2,1)S(1)}, bf16[1,128,3584]{2,1,0:T(8,128)(2,1)}, u32[]{:S(2)}) copy-start(bf16[1,128,3584]{2,1,0:T(8,128)(2,1)} %up_ref.1) | copy-start | bytes 2752516
  0.7 19.9 %copy-start.2 = (bf16[1,128,3584]{2,1,0:T(8,128)(2,1)S(1)}, bf16[1,128,3584]{2,1,0:T(8,128)(2,1)}, u32[]{:S(2)}) copy-start(bf16[1,128,3584]{2,1,0:T(8,128)(2,1)} %down_ref.1) | copy-start | bytes 2752516
  19.0 1.5 %collective-permute-start = (bf16[16,56,128]{2,1,0:T(8,128)(2,1)S(1)}, bf16[16,56,128]{2,1,0:T(8,128)(2,1)S(1)}, u32[]{:S(2)}, u32[]{:S(2)}) collective-permute-start(bf16[16,56,128]{2,1,0:T(8,128)(2,1)S(1)} %all_to_all.10.mine_ref), channel_id=1, source_target_pairs={{0,1},{1,0},{2,3},{3,2},{4,5},{5,4},{6,7},{7,6},{8,9},{9,8},{10,11... | collective-permute-start | bytes 688136 | tf_op jit(solution)/shard_map/ppermute | solution.py:161
  23.0 12.4 %all-to-all-start.1 = ((bf16[32,7,4,128]{3,2,1,0:T(4,128)(2,1)}), bf16[32,7,4,128]{3,2,1,0:T(4,128)(2,1)S(1)}, u32[]{:S(2)}, u32[]{:S(2)}) async-start(bf16[32,7,4,128]{3,2,1,0:T(4,128)(2,1)} %bitcast.1), calls=%async_computation.1 | async-start | bytes 458752 | tf_op jit(solution)/shard_map/all_to_all | solution.py:245
